TPU v7x, 128 devices: a whole 4x4x4 slice. The times are simulated.
128 devices in a mesh: blk: 16 (over x, z_lo, core), dp: 8 (over y, z_hi).
Axes of the slice: x: 4, y: 4, z: 4 (z_hi: 2, z_lo: 2; z = z_hi * 2 + z_lo), core: 2. Of those that a mesh axis runs over, the one named last changes fastest.
Arguments:
- x_in: bfloat16 [196608, 896], P(('blk', 'dp')), may hold values from -6 to 6
- cotangent: bfloat16 [98304, 896], P(('blk', 'dp')), may hold values from -0.059814453 to 0.059814453
- seq_len: int32 [16, 8, 8], P('blk'), may hold values from 36 to 204, as said below
- seq_owner: int32 [16, 8, 8], P('blk'), may hold values from 0 to 7, as said below
- proj_master: float32 [2, 896, 2432], P(None, 'dp', 'blk'), may hold values from -0.1875 to 0.1875
- down_master: float32 [2432, 896], P('blk', 'dp'), may hold values from -0.125 to 0.125
- proj_m: float32 [2, 896, 2432], P(None, 'dp', 'blk'), may hold values from -6 to 6
- proj_v: float32 [2, 896, 2432], P(None, 'dp', 'blk'), may hold values from 0.25 to 4
- down_m: float32 [2432, 896], P('blk', 'dp'), may hold values from -6 to 6
- down_v: float32 [2432, 896], P('blk', 'dp'), may hold values from 0.25 to 4
Outputs:
- mixed: bfloat16 [98304, 896], P(('blk', 'dp'))
- new_proj: float32 [2, 896, 2432], P(None, 'dp', 'blk')
- new_down: float32 [2432, 896], P('blk', 'dp')
- new_proj_m: float32 [2, 896, 2432], P(None, 'dp', 'blk')
- new_proj_v: float32 [2, 896, 2432], P(None, 'dp', 'blk')
- new_down_m: float32 [2432, 896], P('blk', 'dp')
- new_down_v: float32 [2432, 896], P('blk', 'dp')
Inputs may be any that keep to these rules, and one draw needn't show every extreme that they name: `seq_len`: row [b, g] lists the token counts of the 8 sequences held by dp index g of blk index b, packed in order from its first row; one device of each blk index fills all 1536 rows; some count equals 204 in every draw; the sequences sent to each dp index of a blk index hold exactly 768 tokens together. Row [b, g] is a permutation of the dp indices: sequence k of dp index g goes to dp index seq_owner[b, g, k] of the same blk index.
All inputs are finite; a program needn't handle non-finite values.
Results may differ from a plain program's by a relative error of at most 0.015.
Values may be sent and summed in bfloat16 or wider, within the bound.
No kernel may reach another device: no remote copies, remote signals or barrier semaphores. Data moves between devices by JAX's collectives and lax.ppermute only.
A program may use at most 128 MiB of HBM per device.

v0:
```python
import jax
import jax.numpy as jnp
from jax import lax
from jax.experimental import pallas as pl
from jax.experimental.pallas import tpu as pltpu
from jax.sharding import Mesh, PartitionSpec as P

STEP = 100
AXES = ("x", "zl", "c", "y", "zh")
GROUP = ("x", "zl", "y", "zh")
BF = jnp.bfloat16
F32 = jnp.float32
SLOT = 208
WIN = 256
NT = (((1,), (1,)), ((), ()))
MB = 1024 * 1024
SIZE = (26, 12)
LANE = (0, 78)
UNIT = (0, 104)
UNITS = 152
ROWS = tuple(8 * n for n in SIZE)
PART = sum(ROWS)
FIRST = (0, ROWS[0])
STREAMS = len(SIZE)
COLS = STREAMS * 512
HOPS = (2, -1, 1)


def dot(a, b, dims=(((1,), (0,)), ((), ()))):
    return lax.dot_general(a, b, dims, preferred_element_type=F32)


def iota(shape, dim):
    return lax.broadcasted_iota(jnp.int32, shape, dim)


def adam(master, grad, first_moment, second_moment):
    first_new = 0.9 * first_moment + 0.1 * grad
    second_new = 0.95 * second_moment + 0.05 * grad * grad
    first_hat = first_new / (1.0 - 0.9**STEP)
    second_hat = second_new / (1.0 - 0.95**STEP)
    updated = master - 0.0003 * (first_hat / (jnp.sqrt(second_hat) + 1e-08) + 0.1 * master)
    return (updated, first_new, second_new)


VMEM = pl.BlockSpec(memory_space=pltpu.VMEM)
SMEM = pl.BlockSpec(memory_space=pltpu.SMEM)
ANY = pl.BlockSpec(memory_space=pl.ANY)
TB = 256


def params(size):
    return pltpu.CompilerParams(vmem_limit_bytes=size * MB)


def by_stream(index, values):
    out = jnp.full(index.shape, values[0], jnp.int32)
    for s in range(1, STREAMS):
        out = jnp.where(index == s, values[s], out)
    return out


def place(matrix):
    col = iota((1, COLS), 1)
    stream, part, lane = col // 512, (col // 128) % 4, col % 128
    size = by_stream(stream, SIZE)
    i = lane - by_stream(stream, LANE) - matrix * size
    target = jnp.where((i >= 0) & (i < size), by_stream(stream, UNIT) + size * part + i, -1)
    return (iota((UNITS, COLS), 0) == target).astype(F32).astype(BF)


def assemble(stream):
    size, rows = SIZE[stream], 3 * ROWS[stream]
    row = iota((rows, 1), 0)
    matrix = (row >= 8 * size).astype(jnp.int32) + (row >= 16 * size).astype(jnp.int32)
    out = []
    for block in range(8):
        i = row - matrix * 8 * size - block * size
        target = jnp.where((i >= 0) & (i < size), LANE[stream] + matrix * size + i, -1)
        out.append((iota((rows, 128), 1) == target).astype(F32).astype(BF))
    return jnp.concatenate(out, axis=1)


def others():
    return [
        (((x * 2 + zl) * 4 + y) * 2 + zh, x, y, zh * 2 + zl)
        for x in range(4)
        for zl in range(2)
        for y in range(4)
        for zh in range(2)
    ]


def pack_kernel(
    me_ref, core_ref, len_ref, own_ref, x_ref, proj_ref, down_ref, slots_ref, out_ref,
    rows_ref, proj, down, parts, slots, lens, owns, starts, sems, out_sems,
):
    pairs = (
        (proj_ref, proj), (down_ref, down), (len_ref, lens), (own_ref, owns), (x_ref, rows_ref),
    )
    copies = [pltpu.make_async_copy(a, b, sems.at[k]) for k, (a, b) in enumerate(pairs)]
    for copy in copies:
        copy.start()
    d = down.shape[1]
    eye = (iota((d, d), 0) == iota((d, d), 1)).astype(BF)
    total = jnp.zeros((d, COLS), F32)
    for copy in copies[:2]:
        copy.wait()
    for k in range(3):
        m = (down[...] if k == 2 else proj[k]).astype(BF)
        turned = dot(eye, m, NT).astype(BF)
        total = total + dot(turned, place(k))
    total = total.astype(BF)
    for k in range(4 * STREAMS):
        parts[k] = total[:, k * 128 : (k + 1) * 128]
    core = core_ref[0]

    def messages(x, _):
        for k in range(16):
            zl, y, zh = k // 8, (k // 2) % 4, k % 2
            along = jnp.where(core == 0, x, zh * 2 + zl)
            out_ref[x * 16 + k] = parts[along] + parts[4 + y]
        return 0

    lax.fori_loop(0, 4, messages, 0)
    copies[2].wait()
    copies[3].wait()
    n = lens.shape[1]
    rows = rows_ref.shape[0]
    me = me_ref[0]
    first = jnp.int32(0)
    for k in range(n):
        starts[owns[me, k]] = first
        first = first + lens[me, k]
    copies[4].wait()

    def send(g):
        return pltpu.make_async_copy(slots.at[g], slots_ref.at[g], out_sems.at[g])

    def fill(g, _):
        begin = starts[g]
        base = pl.multiple_of(jnp.minimum((begin // 16) * 16, rows - WIN), 16)
        hot = (iota((SLOT, WIN), 1) - iota((SLOT, WIN), 0) == begin - base).astype(BF)
        slots[g] = dot(hot, rows_ref[pl.ds(base, WIN), :]).astype(BF)
        send(g).start()
        return 0

    for g in range(n):
        fill(g, 0)
    for g in range(n):
        send(g).wait()


def pack(me, core, seq_len, seq_owner, x_in, proj, down):
    n = seq_len.shape[0]
    slots = (n, SLOT, x_in.shape[1])
    return pl.pallas_call(
        pack_kernel,
        out_shape=(
            jax.ShapeDtypeStruct(slots, BF),
            jax.ShapeDtypeStruct((64, down.shape[1], 128), BF),
        ),
        in_specs=[SMEM] * 2 + [ANY] * 5,
        out_specs=(ANY, VMEM),
        scratch_shapes=[
            pltpu.VMEM(x_in.shape, BF),
            pltpu.VMEM(proj.shape, F32),
            pltpu.VMEM(down.shape, F32),
            pltpu.VMEM((4 * STREAMS, down.shape[1], 128), BF),
            pltpu.VMEM(slots, BF),
            pltpu.SMEM((n, n), jnp.int32),
            pltpu.SMEM((n, n), jnp.int32),
            pltpu.SMEM((n,), jnp.int32),
            pltpu.SemaphoreType.DMA((5,)),
            pltpu.SemaphoreType.DMA((n,)),
        ],
        compiler_params=params(58),
    )(me, core, seq_len, seq_owner, x_in, proj, down)


def unpack_kernel(me_ref, len_ref, own_ref, slots_ref, cot_ref, after_ref, out_ref, acc_ref):
    n = len_ref.shape[0]
    rows = out_ref.shape[1]
    me = me_ref[0]
    acc_ref[...] = jnp.zeros_like(acc_ref)

    def place_rows(g, at):
        count = jnp.int32(0)
        for k in range(n):
            count = count + jnp.where(own_ref[g, k] == me, len_ref[g, k], 0)
        base = pl.multiple_of((at // 16) * 16, 16)
        row, col = iota((WIN, SLOT), 0), iota((WIN, SLOT), 1)
        sel = ((row - col == at - base) & (col < count)).astype(BF)
        acc_ref[pl.ds(base, WIN), :] += dot(sel, slots_ref[g]).astype(BF)
        return at + count

    at = jnp.int32(0)
    for g in range(n):
        at = place_rows(g, at)
    out_ref[0] = acc_ref[:rows, :]
    out_ref[1] = cot_ref[...]


def unpack(me, seq_len, seq_owner, slots, cot, after):
    rows, d = cot.shape
    return pl.pallas_call(
        unpack_kernel,
        out_shape=jax.ShapeDtypeStruct((2, rows, d), BF),
        in_specs=[SMEM, SMEM, SMEM, VMEM, VMEM, ANY],
        out_specs=VMEM,
        scratch_shapes=[pltpu.VMEM((rows + WIN, d), BF)],
        compiler_params=params(24),
    )(me, seq_len, seq_owner, slots, cot, after)


def turn_kernel(a_ref, b_ref, nrm_ref, nrm_t_ref, cot_ref, cot_t_ref, sel_ref):
    for s in range(STREAMS):
        sel_ref[3 * FIRST[s] : 3 * FIRST[s] + 3 * ROWS[s], :] = assemble(s)
    sel_ref[3 * PART :, :] = jnp.zeros((1024 - 3 * PART, 1024), BF)
    rows = a_ref.shape[1]
    for half, ref in enumerate((a_ref, b_ref)):

        def body(i, _):
            src = pl.ds(pl.multiple_of(i * TB, TB), TB)
            at = pl.ds(pl.multiple_of(half * rows + i * TB, TB), TB)
            t = ref[0, src, :].astype(F32)
            scale = lax.rsqrt(jnp.mean(t * t, axis=1, keepdims=True) + 1e-06)
            t = (t * scale).astype(BF)
            nrm_ref[at, :] = t
            nrm_t_ref[:, at] = t.T
            c = ref[1, src, :]
            cot_ref[at, :] = c
            cot_t_ref[:, at] = c.T
            return 0

        lax.fori_loop(0, rows // TB, body, 0)


def turn(a, b):
    _, rows, d = a.shape
    flat, turned = jax.ShapeDtypeStruct((2 * rows, d), BF), jax.ShapeDtypeStruct((d, 2 * rows), BF)
    return pl.pallas_call(
        turn_kernel,
        out_shape=(flat, turned, flat, turned, jax.ShapeDtypeStruct((1024, 1024), BF)),
        in_specs=[VMEM] * 2,
        out_specs=(VMEM,) * 5,
        compiler_params=params(30),
    )(a, b)


def assemble_kernel(a_ref, *out_refs):
    wide = jnp.concatenate([a_ref[b] for b in range(8)], axis=1)
    for s, out in enumerate(out_refs):
        out[...] = dot(assemble(s), wide, NT).astype(BF)


def assemble_weights(a):
    d = a.shape[1]
    return pl.pallas_call(
        assemble_kernel,
        out_shape=tuple(jax.ShapeDtypeStruct((3 * n, d), BF) for n in ROWS),
        in_specs=[VMEM],
        out_specs=(VMEM,) * STREAMS,
        compiler_params=params(24),
    )(a)


def part_kernel(
    nrm, nrm_t, cot, cot_t, wx, wy, *refs,
):
    gx, gy, hid, w, back = refs[-5:]
    total = nrm.shape[0]
    for s, src in enumerate((wx, wy)):
        n = ROWS[s]
        for m in range(3):
            w[m * PART + FIRST[s] : m * PART + FIRST[s] + n, :] = src[m * n : (m + 1) * n, :]

    def body(i, _):
        at = pl.ds(pl.multiple_of(i * TB, TB), TB)
        gu = dot(w[: 2 * PART, :], nrm_t[:, at])
        dh = dot(w[2 * PART :, :], cot_t[:, at])
        g, u = gu[:PART], gu[PART:]
        s = 0.5 * jnp.tanh(0.5 * g) + 0.5
        silu = g * s
        h = (silu * u).astype(BF)
        back[:PART, at] = (dh * u * s * (1.0 + g * (1.0 - s))).astype(BF)
        back[PART : 2 * PART, at] = (dh * silu).astype(BF)
        back[2 * PART :, at] = h
        hid[:, at] = h
        return 0

    lax.fori_loop(0, total // TB, body, 0, unroll=3)
    w[: 2 * PART, :] = dot(back[: 2 * PART, :], nrm[...]).astype(BF)
    w[2 * PART :, :] = dot(back[2 * PART :, :], cot[...]).astype(BF)
    for s, dst in enumerate((gx, gy)):
        n = ROWS[s]
        for m in range(3):
            dst[m * n : (m + 1) * n, :] = w[m * PART + FIRST[s] : m * PART + FIRST[s] + n, :]


def one_part(nrm, nrm_t, cot, cot_t, weights, after):
    total, d = nrm.shape
    out = pl.pallas_call(
        part_kernel,
        out_shape=tuple(jax.ShapeDtypeStruct((3 * n, d), BF) for n in ROWS)
        + (jax.ShapeDtypeStruct((PART, total), BF),),
        in_specs=[VMEM] * (4 + STREAMS) + [ANY] * len(after),
        out_specs=(VMEM,) * (STREAMS + 1),
        scratch_shapes=[pltpu.VMEM((3 * PART, d), BF), pltpu.VMEM((3 * PART, total), BF)],
        compiler_params=params(28),
        cost_estimate=pl.CostEstimate(
            flops=200_000_000, bytes_accessed=400_000, transcendentals=10_000
        ),
    )(nrm, nrm_t, cot, cot_t, *weights, *after)
    return out[:STREAMS], out[STREAMS]


def mix_kernel(tok_ref, *refs):
    hids, weights, (own_ref, far_ref), (hid, wd, tok, sems) = (
        refs[:4], refs[4:12], refs[12:14], refs[14:],
    )
    rows = own_ref.shape[0]
    copies = [(tok_ref.at[0], tok)]
    for k in range(4):
        copies.append((hids[k], hid.at[k * PART : (k + 1) * PART]))
        for s in range(STREAMS):
            n, at = ROWS[s], k * PART + FIRST[s]
            copies.append((weights[STREAMS * k + s].at[2 * n : 3 * n], wd.at[at : at + n]))
    copies = [pltpu.make_async_copy(a, b, sems.at[i]) for i, (a, b) in enumerate(copies)]
    for copy in copies:
        copy.start()
    for copy in copies:
        copy.wait()

    def body(i, _):
        near = pl.ds(pl.multiple_of(i * TB, TB), TB)
        far = pl.ds(pl.multiple_of(rows + i * TB, TB), TB)
        own_ref[near, :] = dot(hid[:, near].T, wd[...]) + tok[near, :].astype(F32)
        far_ref[near, :] = dot(hid[:, far].T, wd[...]).astype(BF)
        return 0

    lax.fori_loop(0, rows // TB, body, 0)


def mix(tok, hids, weights):
    _, rows, d = tok.shape
    return pl.pallas_call(
        mix_kernel,
        out_shape=(jax.ShapeDtypeStruct((rows, d), F32), jax.ShapeDtypeStruct((rows, d), BF)),
        in_specs=[ANY] * 13,
        out_specs=(VMEM,) * 2,
        scratch_shapes=[
            pltpu.VMEM((4 * PART, 2 * rows), BF),
            pltpu.VMEM((4 * PART, d), BF),
            pltpu.VMEM((rows, d), BF),
            pltpu.SemaphoreType.DMA((13,)),
        ],
        compiler_params=params(60),
        cost_estimate=pl.CostEstimate(
            flops=3_500_000_000, bytes_accessed=16_000_000, transcendentals=0
        ),
    )(tok, *hids, *[w for part in weights for w in part])


def pack_grads_kernel(*refs):
    sel_ref, out_ref, rows_ref = refs[4 * STREAMS :]
    d = out_ref.shape[1]
    for s in range(STREAMS):
        total = refs[s][...].astype(F32)
        for k in range(1, 4):
            total = total + refs[STREAMS * k + s][...].astype(F32)
        rows_ref[3 * FIRST[s] : 3 * FIRST[s] + 3 * ROWS[s], :] = total.astype(BF)
    rows_ref[3 * PART :, :] = jnp.zeros((1024 - 3 * PART, d), BF)
    turned = rows_ref[...].T
    for b in range(0, 8, 2):
        pair = dot(turned, sel_ref[:, b * 128 : (b + 2) * 128]).astype(BF)
        for k in range(2):
            out_ref[b + k] = pair[:, k * 128 : (k + 1) * 128]


def pack_grads(parts, sel):
    d = parts[0][0].shape[1]
    return pl.pallas_call(
        pack_grads_kernel,
        out_shape=jax.ShapeDtypeStruct((8, d, 128), BF),
        in_specs=[VMEM] * (4 * STREAMS + 1),
        out_specs=VMEM,
        scratch_shapes=[pltpu.VMEM((1024, d), BF)],
        compiler_params=params(40),
    )(*[g for part in parts for g in part], sel)


def update_kernel(core_ref, a_ref, *refs):
    (proj, proj_m, proj_v, down, down_m, down_v), outs, (wide_ref,) = (
        refs[:6], refs[6:12], refs[12:],
    )
    sums = [[None] * 4 for _ in range(3)]
    for index, *place_of in others():
        v = a_ref[index].astype(F32)
        for s, p in enumerate(place_of):
            sums[s][p] = v if sums[s][p] is None else sums[s][p] + v
    for p in range(4):
        wide_ref[:, p * 128 : (p + 1) * 128] = jnp.where(core_ref[0] == 0, sums[0][p], sums[2][p])
        wide_ref[:, 512 + p * 128 : 512 + (p + 1) * 128] = sums[1][p]
    wide = wide_ref[...]
    high = wide.astype(BF)
    low = (wide - high.astype(F32)).astype(BF)
    for k in range(3):
        sel = place(k)
        grad = dot(sel, high, NT) + dot(sel, low, NT)
        if k < 2:
            new = adam(proj[k], grad, proj_m[k], proj_v[k])
            for out, v in zip(outs[:3], new):
                out[k] = v
        else:
            new = adam(down[...], grad, down_m[...], down_v[...])
            for out, v in zip(outs[3:], new):
                out[...] = v


def update(core, pieces, proj, proj_m, proj_v, down, down_m, down_v):
    shape = lambda a: jax.ShapeDtypeStruct(a.shape, F32)
    return pl.pallas_call(
        update_kernel,
        out_shape=(shape(proj),) * 3 + (shape(down),) * 3,
        in_specs=[SMEM] + [VMEM] * 7,
        out_specs=(VMEM,) * 6,
        scratch_shapes=[pltpu.VMEM((down.shape[1], COLS), F32)],
        compiler_params=params(24),
    )(core, pieces, proj, proj_m, proj_v, down, down_m, down_v)


def shift_pairs(sizes, stream, hops):
    pairs = []
    nx, nzl, nc, ny, nzh = sizes
    line = lambda x, zl, c, y, zh: (((x * nzl + zl) * nc + c) * ny + y) * nzh + zh
    for x in range(nx):
        for zl in range(nzl):
            for c in range(nc):
                for y in range(ny):
                    for zh in range(nzh):
                        to = [x, y, zh * nzl + zl]
                        axis = 1 if stream else (0, 2)[c]
                        step = -hops if c else hops
                        to[axis] = (to[axis] + step) % (nx, ny, nzh * nzl)[axis]
                        pairs.append(
                            (
                                line(x, zl, c, y, zh),
                                line(to[0], to[2] % nzl, c, to[1], to[2] // nzl),
                            )
                        )
    return pairs


def shifted(parts, hops):
    sizes = tuple(lax.axis_size(a) for a in AXES)
    return tuple(
        lax.ppermute(v, AXES, shift_pairs(sizes, stream, hops)) for stream, v in enumerate(parts)
    )


def swap_cores(v):
    return lax.ppermute(v, "c", [(0, 1), (1, 0)])


def per_device(
    x_in, cotangent, seq_len, seq_owner, proj_master, down_master, proj_m, proj_v, down_m, down_v
):
    rows, d = cotangent.shape
    me = (lax.axis_index("y") * lax.axis_size("zh") + lax.axis_index("zh")).reshape(1)
    core = lax.axis_index("c").reshape(1)
    counts, owners = seq_len[0], seq_owner[0]
    flip = lambda v: jnp.swapaxes(v, 1, 2)
    slots, packed = pack(me, core, counts, owners, x_in, flip(proj_master), down_master)
    slots = lax.all_to_all(slots, ("y", "zh"), 0, 0, tiled=True)
    packed, slots = lax.optimization_barrier((packed, slots))
    arrived = lax.all_to_all(packed, GROUP, 0, 0, tiled=True)
    own = assemble_weights(arrived.reshape(8, d, 128))
    near_in = unpack(me, counts, owners, slots, cotangent, own[0])
    *acts, rows_of = turn(near_in, swap_cores(near_in))
    weights = [shifted(own, -k) for k in HOPS] + [own]
    sums, hids, after = [], [], [near_in]
    for i, w in enumerate(weights):
        if i == 2:
            after += sums[0][1:]
        g, h = one_part(*acts, w, after)
        sums.append(shifted(g, HOPS[i]) if i < 3 else g)
        hids.append(h)
        after = [h]
    messages = pack_grads(sums, rows_of).reshape(64, d // 8, 128)
    pieces = lax.all_to_all(messages, GROUP, 0, 0, tiled=True)
    near, far = mix(near_in, hids, weights)
    mixed = (near + swap_cores(far).astype(F32)).astype(BF)
    out = update(
        core, pieces, flip(proj_master), flip(proj_m), flip(proj_v), down_master, down_m, down_v
    )
    new_proj, new_proj_m, new_proj_v = (flip(v) for v in out[:3])
    new_down, new_down_m, new_down_v = out[3:]
    return (mixed, new_proj, new_down, new_proj_m, new_proj_v, new_down_m, new_down_v)


def solution(mesh):
    mesh = Mesh(mesh.devices.reshape(4, 2, 2, 4, 2), AXES)
    blk, dp = ("x", "zl", "c"), ("y", "zh")
    in_specs = (
        P(blk + dp, None),
        P(blk + dp, None),
        P(blk, None, None),
        P(blk, None, None),
        P(None, dp, blk),
        P(blk, dp),
        P(None, dp, blk),
        P(None, dp, blk),
        P(blk, dp),
        P(blk, dp),
    )
    out_specs = (
        P(blk + dp, None),
        P(None, dp, blk),
        P(blk, dp),
        P(None, dp, blk),
        P(None, dp, blk),
        P(blk, dp),
        P(blk, dp),
    )
    return jax.shard_map(
        per_device, mesh=mesh, in_specs=in_specs, out_specs=out_specs, check_vma=False
    )
```

profile of v0, /device:TPU:0, one launch (start us, length us, event | category | flops | bytes accessed | tf_op | source)
XLA Modules:
  0.0 191.9 jit_solution(6121997430729535774)
XLA Ops:
  0.6 5.2 %shard_map.153 = (bf16[8,208,896]{2,1,0:T(8,128)(2,1)}, bf16[64,112,128]{2,1,0:T(8,128)(2,1)}) custom-call(s32[1]{0:T(128)} %bitcast.me_ref, s32[1]{0:T(128)} %bitcast.3.core_ref, s32[8,8]{1,0:T(8,128)} %bitcast.17, s32[8,8]{1,0:T(8,128)} %bitcast.19, bf16[1536,896]{1,0:T(8,128)(2,1)} %x_ref.1, f32[2,152,112]{2,1,0:T(8,128)} %bitcast.13, f32[152,112]{1,0:T(8,128)} %refs_3_.1), custom_call_target="tpu_custom_call" | custom-call | tf_op jit(solution)/shard_map/pallas_call | solution.py:157
  5.8 46.2 %all_to_all.15.slots_ref = bf16[8,208,896]{2,1,0:T(8,128)(2,1)S(1)} all-to-all(bf16[8,208,896]{2,1,0:T(8,128)(2,1)} %get-tuple-element.39), channel_id=1, replica_groups=mesh['x'=4,'zl'=2,'c'=2,'y'=4,'zh'=2] {'y','zh'}, dimensions={0} | all-to-all | bytes 5963776 | tf_op jit(solution)/shard_map/all_to_all | solution.py:475
  52.0 32.2 %all_to_all.16 = bf16[64,112,128]{2,1,0:T(8,128)(2,1)S(1)} all-to-all(bf16[64,112,128]{2,1,0:T(8,128)(2,1)S(1)} %copy-done.24), channel_id=1, replica_groups=mesh['x'=4,'zl'=2,'c'=2,'y'=4,'zh'=2] {'x','zl','y','zh'}, dimensions={0} | all-to-all | bytes 3670016 | tf_op jit(solution)/shard_map/all_to_all | solution.py:477
  84.3 2.1 %shard_map.154 = (bf16[624,896]{1,0:T(8,128)(2,1)S(1)}, bf16[288,896]{1,0:T(8,128)(2,1)S(1)}) custom-call(bf16[8,896,128]{2,1,0:T(8,128)(2,1)S(1)} %bitcast.12), custom_call_target="tpu_custom_call" | custom-call | tf_op jit(solution)/shard_map/pallas_call | solution.py:259
  86.5 2.2 %shard_map.155.a_ref.refs_0_.tok_ref = bf16[2,768,896]{2,1,0:T(8,128)(2,1)S(1)} custom-call(s32[1]{0:T(128)} %bitcast.me_ref, s32[8,8]{1,0:T(8,128)S(1)} %bitcast.18, s32[8,8]{1,0:T(8,128)S(1)} %bitcast.20, bf16[8,208,896]{2,1,0:T(8,128)(2,1)S(1)} %all_to_all.15.slots_ref, bf16[768,896]{1,0:T(8,128)(2,1)S(1)} %copy-done.14, ...), custom_call_target="tpu_custom_call" | custom-call | tf_op jit(solution)/shard_map/pallas_call | solution.py:206
  88.8 0.7 collective-permute-start.1
  89.6 1.3 collective-permute-start.3
  90.8 2.0 %collective-permute-start.5 = (bf16[624,896]{1,0:T(8,128)(2,1)S(1)}, bf16[624,896]{1,0:T(8,128)(2,1)S(1)}, u32[]{:S(2)}, u32[]{:S(2)}) collective-permute-start(bf16[624,896]{1,0:T(8,128)(2,1)S(1)} %get-tuple-element.42.after_ref.wx.refs_10_), channel_id=1, source_target_pairs={{0,96},{1,97},{2,98},{3,99},{4,100},{5,101},{6,102},{7,103},{8,24}... | collective-permute-start | bytes 3354632 | tf_op jit(solution)/shard_map/ppermute | solution.py:458
  92.8 1.6 collective-permute-start.2
  94.4 0.8 collective-permute-start.4
  95.2 2.7 %shard_map.156 = (bf16[1536,896]{1,0:T(8,128)(2,1)S(1)}, bf16[896,1536]{1,0:T(8,128)(2,1)S(1)}, bf16[1536,896]{1,0:T(8,128)(2,1)S(1)}, bf16[896,1536]{1,0:T(8,128)(2,1)S(1)}, bf16[1024,1024]{1,0:T(8,128)(2,1)S(1)}) custom-call(bf16[2,768,896]{2,1,0:T(8,128)(2,1)S(1)} %shard_map.155.a_ref.refs_0_.tok_ref, bf16[2,768,896]{2,1,0:T(8,128)(2,1)S(1)} %collective-permute-done.b_ref), custom_call_target="tpu_custom_call" | custom-call | tf_op jit(solution)/shard_map/pallas_call | solution.py:242
  97.9 8.8 %collective-permute-done.2.wy.refs_5_ = bf16[288,896]{1,0:T(8,128)(2,1)S(1)} collective-permute-done((bf16[288,896]{1,0:T(8,128)(2,1)S(1)}, bf16[288,896]{1,0:T(8,128)(2,1)S(1)}, u32[]{:S(2)}, u32[]{:S(2)}) %collective-permute-start.2) | collective-permute-done | bytes 516128 | tf_op jit(solution)/shard_map/ppermute | solution.py:458
  106.7 3.9 %collective-permute-start.6 = (bf16[288,896]{1,0:T(8,128)(2,1)S(1)}, bf16[288,896]{1,0:T(8,128)(2,1)S(1)}, u32[]{:S(2)}, u32[]{:S(2)}) collective-permute-start(bf16[288,896]{1,0:T(8,128)(2,1)S(1)} %get-tuple-element.47.wy.refs_11_), channel_id=1, source_target_pairs={{0,6},{1,7},{2,0},{3,1},{4,2},{5,3},{6,4},{7,5},{8,10},{9,11},{10,... | collective-permute-start | bytes 1548296 | tf_op jit(solution)/shard_map/ppermute | solution.py:458
  110.6 6.7 %shard_map.157 = (bf16[624,896]{1,0:T(8,128)(2,1)S(1)}, bf16[288,896]{1,0:T(8,128)(2,1)S(1)}, bf16[304,1536]{1,0:T(8,128)(2,1)S(1)}) custom-call(bf16[1536,896]{1,0:T(8,128)(2,1)S(1)} %get-tuple-element.43.nrm, bf16[896,1536]{1,0:T(8,128)(2,1)S(1)} %get-tuple-element.44.nrm_t, bf16[1536,896]{1,0:T(8,128)(2,1)S(1)} %get-tuple-element.45.cot, ...), custom_call_target="tpu_custom_call" | custom-call | flops 200000000 | bytes 400000 | tf_op jit(solution)/shard_map/pallas_call | solution.py:303
  117.3 1.4 collective-permute-start.7
  118.7 1.4 collective-permute-start.9
  120.1 6.7 %shard_map.158 = (bf16[624,896]{1,0:T(8,128)(2,1)S(1)}, bf16[288,896]{1,0:T(8,128)(2,1)S(1)}, bf16[304,1536]{1,0:T(8,128)(2,1)S(1)}) custom-call(bf16[1536,896]{1,0:T(8,128)(2,1)S(1)} %get-tuple-element.43.nrm, bf16[896,1536]{1,0:T(8,128)(2,1)S(1)} %get-tuple-element.44.nrm_t, bf16[1536,896]{1,0:T(8,128)(2,1)S(1)} %get-tuple-element.45.cot, ...), custom_call_target="tpu_custom_call" | custom-call | flops 200000000 | bytes 400000 | tf_op jit(solution)/shard_map/pallas_call | solution.py:303
  126.8 1.2 collective-permute-start.10
  128.3 0.5 collective-permute-done.7.refs_1_
  128.7 6.7 %shard_map.159 = (bf16[624,896]{1,0:T(8,128)(2,1)S(1)}, bf16[288,896]{1,0:T(8,128)(2,1)S(1)}, bf16[304,1536]{1,0:T(8,128)(2,1)S(1)}) custom-call(bf16[1536,896]{1,0:T(8,128)(2,1)S(1)} %get-tuple-element.43.nrm, bf16[896,1536]{1,0:T(8,128)(2,1)S(1)} %get-tuple-element.44.nrm_t, bf16[1536,896]{1,0:T(8,128)(2,1)S(1)} %get-tuple-element.45.cot, ...), custom_call_target="tpu_custom_call" | custom-call | flops 200000000 | bytes 400000 | tf_op jit(solution)/shard_map/pallas_call | solution.py:303
  135.8 3.0 %collective-permute-start.11 = (bf16[288,896]{1,0:T(8,128)(2,1)S(1)}, bf16[288,896]{1,0:T(8,128)(2,1)S(1)}, u32[]{:S(2)}, u32[]{:S(2)}) collective-permute-start(bf16[288,896]{1,0:T(8,128)(2,1)S(1)} %get-tuple-element.57), channel_id=1, source_target_pairs={{0,6},{1,7},{2,0},{3,1},{4,2},{5,3},{6,4},{7,5},{8,10},{9,11},{10,... | collective-permute-start | bytes 1548296 | tf_op jit(solution)/shard_map/ppermute | solution.py:458
  138.8 6.7 %shard_map.160 = (bf16[624,896]{1,0:T(8,128)(2,1)S(1)}, bf16[288,896]{1,0:T(8,128)(2,1)S(1)}, bf16[304,1536]{1,0:T(8,128)(2,1)S(1)}) custom-call(bf16[1536,896]{1,0:T(8,128)(2,1)S(1)} %get-tuple-element.43.nrm, bf16[896,1536]{1,0:T(8,128)(2,1)S(1)} %get-tuple-element.44.nrm_t, bf16[1536,896]{1,0:T(8,128)(2,1)S(1)} %get-tuple-element.45.cot, ...), custom_call_target="tpu_custom_call" | custom-call | flops 200000000 | bytes 400000 | tf_op jit(solution)/shard_map/pallas_call | solution.py:303
  145.5 0.9 copy-done.15
  146.5 3.8 %collective-permute-done.11.refs_3_ = bf16[288,896]{1,0:T(8,128)(2,1)S(1)} collective-permute-done((bf16[288,896]{1,0:T(8,128)(2,1)S(1)}, bf16[288,896]{1,0:T(8,128)(2,1)S(1)}, u32[]{:S(2)}, u32[]{:S(2)}) %collective-permute-start.11) | collective-permute-done | bytes 516128 | tf_op jit(solution)/shard_map/ppermute | solution.py:458
  150.3 2.2 %collective-permute-done.13.refs_5_ = bf16[288,896]{1,0:T(8,128)(2,1)S(1)} collective-permute-done((bf16[288,896]{1,0:T(8,128)(2,1)S(1)}, bf16[288,896]{1,0:T(8,128)(2,1)S(1)}, u32[]{:S(2)}, u32[]{:S(2)}) %collective-permute-start.13) | collective-permute-done | bytes 516128 | tf_op jit(solution)/shard_map/ppermute | solution.py:458
  152.5 3.5 %shard_map.162 = bf16[8,896,128]{2,1,0:T(8,128)(2,1)} custom-call(bf16[624,896]{1,0:T(8,128)(2,1)S(1)} %collective-permute-done.9.refs_0_, bf16[288,896]{1,0:T(8,128)(2,1)S(1)} %collective-permute-done.7.refs_1_, bf16[624,896]{1,0:T(8,128)(2,1)S(1)} %collective-permute-done.10.refs_2_, bf16[288,896]{1,0:T(8,128)(2,1)S(1)} %collective-permute-done.11.refs_3_, ...), custom_call_target="tpu_custom_call" | custom-call | tf_op jit(solution)/shard_map/pallas_call | solution.py:383
  156.0 7.2 %all-to-all-start.2 = ((bf16[64,112,128]{2,1,0:T(8,128)(2,1)}), bf16[64,112,128]{2,1,0:T(8,128)(2,1)S(1)}, u32[]{:S(2)}, u32[]{:S(2)}) async-start(bf16[64,112,128]{2,1,0:T(8,128)(2,1)} %bitcast.6), calls=%async_computation.2 | async-start | bytes 3670016 | tf_op jit(solution)/shard_map/all_to_all | solution.py:491
  163.1 9.2 %shard_map.161 = (f32[768,896]{1,0:T(8,128)}, bf16[768,896]{1,0:T(8,128)(2,1)}) custom-call(bf16[2,768,896]{2,1,0:T(8,128)(2,1)} %copy-done, bf16[304,1536]{1,0:T(8,128)(2,1)} %copy-done.5, bf16[304,1536]{1,0:T(8,128)(2,1)} %copy-done.6, bf16[304,1536]{1,0:T(8,128)(2,1)} %copy-done.7, bf16[304,1536]{1,0:T(8,128)(2,1)} %copy-done.15, ...), custom_call_target="tpu_custom_call" | custom-call | flops 3500000000 | bytes 16000000 | tf_op jit(solution)/shard_map/pallas_call | solution.py:347
  172.4 3.3 %collective-permute-done.8 = bf16[768,896]{1,0:T(8,128)(2,1)S(1)} collective-permute-done((bf16[768,896]{1,0:T(8,128)(2,1)}, bf16[768,896]{1,0:T(8,128)(2,1)S(1)}, u32[]{:S(2)}, u32[]{:S(2)}) %collective-permute-start.8) | collective-permute-done | bytes 1376288 | tf_op jit(solution)/shard_map/ppermute | solution.py:463
  175.8 3.2 %add_convert_fusion = bf16[768,896]{1,0:T(8,128)(2,1)} fusion(f32[768,896]{1,0:T(8,128)} %get-tuple-element.53, bf16[768,896]{1,0:T(8,128)(2,1)S(1)} %collective-permute-done.8), kind=kLoop, calls=%fused_computation | loop fusion | flops 2064384 | bytes 5505024 | tf_op jit(solution)/shard_map/convert_element_type | solution.py:493
  179.0 10.7 %all-to-all-done.2.a_ref = bf16[64,112,128]{2,1,0:T(8,128)(2,1)S(1)} async-done(((bf16[64,112,128]{2,1,0:T(8,128)(2,1)}), bf16[64,112,128]{2,1,0:T(8,128)(2,1)S(1)}, u32[]{:S(2)}, u32[]{:S(2)}) %all-to-all-start.2) | async-done | bytes 1835040 | tf_op jit(solution)/shard_map/all_to_all | solution.py:491
  189.8 2.1 %shard_map.163 = (f32[2,152,112]{2,1,0:T(8,128)}, f32[2,152,112]{2,1,0:T(8,128)}, f32[2,152,112]{2,1,0:T(8,128)}, f32[152,112]{1,0:T(8,128)}, f32[152,112]{1,0:T(8,128)}, /*index=5*/f32[152,112]{1,0:T(8,128)}) custom-call(s32[1]{0:T(128)} %bitcast.3.core_ref, bf16[64,112,128]{2,1,0:T(8,128)(2,1)S(1)} %all-to-all-done.2.a_ref, f32[2,152,112]{2,1,0:T(8,128)S(1)} %bitcast.14, ...), custom_call_target="tpu_custom_call" | custom-call | tf_op jit(solution)/shard_map/pallas_call | solution.py:423
  (62 shorter events, 1.0 us)
Async XLA Ops:
  5.8 46.2 %copy-start.24 = (bf16[64,112,128]{2,1,0:T(8,128)(2,1)S(1)}, bf16[64,112,128]{2,1,0:T(8,128)(2,1)}, u32[]{:S(2)}) copy-start(bf16[64,112,128]{2,1,0:T(8,128)(2,1)} %get-tuple-element.41) | copy-start | bytes 5505028
  86.4 52.4 %copy-start.1 = (bf16[624,896]{1,0:T(8,128)(2,1)}, bf16[624,896]{1,0:T(8,128)(2,1)S(1)}, u32[]{:S(2)}) copy-start(bf16[624,896]{1,0:T(8,128)(2,1)S(1)} %get-tuple-element.42.after_ref.wx.refs_10_) | copy-start | bytes 3354628
  86.4 52.4 %copy-start.10 = (bf16[288,896]{1,0:T(8,128)(2,1)}, bf16[288,896]{1,0:T(8,128)(2,1)S(1)}, u32[]{:S(2)}) copy-start(bf16[288,896]{1,0:T(8,128)(2,1)S(1)} %get-tuple-element.47.wy.refs_11_) | copy-start | bytes 1548292
  88.7 21.9 %copy-start = (bf16[2,768,896]{2,1,0:T(8,128)(2,1)}, bf16[2,768,896]{2,1,0:T(8,128)(2,1)S(1)}, u32[]{:S(2)}) copy-start(bf16[2,768,896]{2,1,0:T(8,128)(2,1)S(1)} %shard_map.155.a_ref.refs_0_.tok_ref) | copy-start | bytes 8257540
  88.7 5.7 %collective-permute-start = (bf16[2,768,896]{2,1,0:T(8,128)(2,1)S(1)}, bf16[2,768,896]{2,1,0:T(8,128)(2,1)S(1)}, u32[]{:S(2)}, u32[]{:S(2)}) collective-permute-start(bf16[2,768,896]{2,1,0:T(8,128)(2,1)S(1)} %shard_map.155.a_ref.refs_0_.tok_ref), channel_id=1, source_target_pairs={{0,8},{8,0},{1,9},{9,1},{2,10},{10,2},{3,11},{11,3},{4,12},{12,4},... | collective-permute-start | bytes 8257544 | tf_op jit(solution)/shard_map/ppermute | solution.py:463
  88.8 21.8 %collective-permute-start.1 = (bf16[624,896]{1,0:T(8,128)(2,1)S(1)}, bf16[624,896]{1,0:T(8,128)(2,1)S(1)}, u32[]{:S(2)}, u32[]{:S(2)}) collective-permute-start(bf16[624,896]{1,0:T(8,128)(2,1)S(1)} %get-tuple-element.42.after_ref.wx.refs_10_), channel_id=1, source_target_pairs={{0,64},{1,65},{2,66},{3,67},{4,68},{5,69},{6,70},{7,71},{8,9},{9,8... | collective-permute-start | bytes 3354632 | tf_op jit(solution)/shard_map/ppermute | solution.py:458
  89.6 30.6 %collective-permute-start.3 = (bf16[624,896]{1,0:T(8,128)(2,1)S(1)}, bf16[624,896]{1,0:T(8,128)(2,1)S(1)}, u32[]{:S(2)}, u32[]{:S(2)}) collective-permute-start(bf16[624,896]{1,0:T(8,128)(2,1)S(1)} %get-tuple-element.42.after_ref.wx.refs_10_), channel_id=1, source_target_pairs={{0,32},{1,33},{2,34},{3,35},{4,36},{5,37},{6,38},{7,39},{8,25},{9,... | collective-permute-start | bytes 3354632 | tf_op jit(solution)/shard_map/ppermute | solution.py:458
  90.8 37.5 %collective-permute-start.5 = (bf16[624,896]{1,0:T(8,128)(2,1)S(1)}, bf16[624,896]{1,0:T(8,128)(2,1)S(1)}, u32[]{:S(2)}, u32[]{:S(2)}) collective-permute-start(bf16[624,896]{1,0:T(8,128)(2,1)S(1)} %get-tuple-element.42.after_ref.wx.refs_10_), channel_id=1, source_target_pairs={{0,96},{1,97},{2,98},{3,99},{4,100},{5,101},{6,102},{7,103},{8,24}... | collective-permute-start | bytes 3354632 | tf_op jit(solution)/shard_map/ppermute | solution.py:458
  92.8 13.9 %collective-permute-start.2 = (bf16[288,896]{1,0:T(8,128)(2,1)S(1)}, bf16[288,896]{1,0:T(8,128)(2,1)S(1)}, u32[]{:S(2)}, u32[]{:S(2)}) collective-permute-start(bf16[288,896]{1,0:T(8,128)(2,1)S(1)} %get-tuple-element.47.wy.refs_11_), channel_id=1, source_target_pairs={{0,4},{1,5},{2,6},{3,7},{4,0},{5,1},{6,2},{7,3},{8,12},{9,13},{10,... | collective-permute-start | bytes 1548296 | tf_op jit(solution)/shard_map/ppermute | solution.py:458
  94.4 24.3 %collective-permute-start.4 = (bf16[288,896]{1,0:T(8,128)(2,1)S(1)}, bf16[288,896]{1,0:T(8,128)(2,1)S(1)}, u32[]{:S(2)}, u32[]{:S(2)}) collective-permute-start(bf16[288,896]{1,0:T(8,128)(2,1)S(1)} %get-tuple-element.47.wy.refs_11_), channel_id=1, source_target_pairs={{0,2},{1,3},{2,4},{3,5},{4,6},{5,7},{6,0},{7,1},{8,14},{9,15},{10,... | collective-permute-start | bytes 1548296 | tf_op jit(solution)/shard_map/ppermute | solution.py:458
  97.9 19.4 %copy-start.8 = (bf16[1024,1024]{1,0:T(8,128)(2,1)}, bf16[1024,1024]{1,0:T(8,128)(2,1)S(1)}, u32[]{:S(2)}) copy-start(bf16[1024,1024]{1,0:T(8,128)(2,1)S(1)} %get-tuple-element.62.refs_8_) | copy-start | bytes 6291460
  106.7 10.6 %copy-start.11 = (bf16[288,896]{1,0:T(8,128)(2,1)}, bf16[288,896]{1,0:T(8,128)(2,1)S(1)}, u32[]{:S(2)}) copy-start(bf16[288,896]{1,0:T(8,128)(2,1)S(1)} %collective-permute-done.2.wy.refs_5_) | copy-start | bytes 1548292
  106.7 21.6 %collective-permute-start.6 = (bf16[288,896]{1,0:T(8,128)(2,1)S(1)}, bf16[288,896]{1,0:T(8,128)(2,1)S(1)}, u32[]{:S(2)}, u32[]{:S(2)}) collective-permute-start(bf16[288,896]{1,0:T(8,128)(2,1)S(1)} %get-tuple-element.47.wy.refs_11_), channel_id=1, source_target_pairs={{0,6},{1,7},{2,0},{3,1},{4,2},{5,3},{6,4},{7,5},{8,10},{9,11},{10,... | collective-permute-start | bytes 1548296 | tf_op jit(solution)/shard_map/ppermute | solution.py:458
  117.3 9.5 %copy-start.5 = (bf16[304,1536]{1,0:T(8,128)(2,1)}, bf16[304,1536]{1,0:T(8,128)(2,1)S(1)}, u32[]{:S(2)}) copy-start(bf16[304,1536]{1,0:T(8,128)(2,1)S(1)} %get-tuple-element.48.refs_0_) | copy-start | bytes 2801668
  117.3 11.4 %collective-permute-start.7 = (bf16[288,896]{1,0:T(8,128)(2,1)S(1)}, bf16[288,896]{1,0:T(8,128)(2,1)S(1)}, u32[]{:S(2)}, u32[]{:S(2)}) collective-permute-start(bf16[288,896]{1,0:T(8,128)(2,1)S(1)} %get-tuple-element.50), channel_id=1, source_target_pairs={{0,4},{1,5},{2,6},{3,7},{4,0},{5,1},{6,2},{7,3},{8,12},{9,13},{10,... | collective-permute-start | bytes 1548296 | tf_op jit(solution)/shard_map/ppermute | solution.py:458
  118.7 8.1 %copy-start.12 = (bf16[288,896]{1,0:T(8,128)(2,1)}, bf16[288,896]{1,0:T(8,128)(2,1)S(1)}, u32[]{:S(2)}) copy-start(bf16[288,896]{1,0:T(8,128)(2,1)S(1)} %collective-permute-done.4.wy.refs_7_) | copy-start | bytes 1548292
  118.7 33.7 %collective-permute-start.9 = (bf16[624,896]{1,0:T(8,128)(2,1)S(1)}, bf16[624,896]{1,0:T(8,128)(2,1)S(1)}, u32[]{:S(2)}, u32[]{:S(2)}) collective-permute-start(bf16[624,896]{1,0:T(8,128)(2,1)S(1)} %get-tuple-element.55), channel_id=1, source_target_pairs={{0,64},{1,65},{2,66},{3,67},{4,68},{5,69},{6,70},{7,71},{8,9},{9,8... | collective-permute-start | bytes 3354632 | tf_op jit(solution)/shard_map/ppermute | solution.py:458
  126.8 8.6 %copy-start.6 = (bf16[304,1536]{1,0:T(8,128)(2,1)}, bf16[304,1536]{1,0:T(8,128)(2,1)S(1)}, u32[]{:S(2)}) copy-start(bf16[304,1536]{1,0:T(8,128)(2,1)S(1)} %get-tuple-element.49.refs_0_.refs_1_) | copy-start | bytes 2801668
  126.8 25.6 %collective-permute-start.10 = (bf16[624,896]{1,0:T(8,128)(2,1)S(1)}, bf16[624,896]{1,0:T(8,128)(2,1)S(1)}, u32[]{:S(2)}, u32[]{:S(2)}) collective-permute-start(bf16[624,896]{1,0:T(8,128)(2,1)S(1)} %get-tuple-element.56), channel_id=1, source_target_pairs={{0,96},{1,97},{2,98},{3,99},{4,100},{5,101},{6,102},{7,103},{8,24}... | collective-permute-start | bytes 3354632 | tf_op jit(solution)/shard_map/ppermute | solution.py:458
  135.4 10.1 %copy-start.7 = (bf16[304,1536]{1,0:T(8,128)(2,1)}, bf16[304,1536]{1,0:T(8,128)(2,1)S(1)}, u32[]{:S(2)}) copy-start(bf16[304,1536]{1,0:T(8,128)(2,1)S(1)} %get-tuple-element.51.refs_0_.refs_2_) | copy-start | bytes 2801668
  135.5 17.0 %collective-permute-start.12 = (bf16[624,896]{1,0:T(8,128)(2,1)S(1)}, bf16[624,896]{1,0:T(8,128)(2,1)S(1)}, u32[]{:S(2)}, u32[]{:S(2)}) collective-permute-start(bf16[624,896]{1,0:T(8,128)(2,1)S(1)} %get-tuple-element.58), channel_id=1, source_target_pairs={{0,32},{1,33},{2,34},{3,35},{4,36},{5,37},{6,38},{7,39},{8,25},{9,... | collective-permute-start | bytes 3354632 | tf_op jit(solution)/shard_map/ppermute | solution.py:458
  135.8 14.4 %collective-permute-start.11 = (bf16[288,896]{1,0:T(8,128)(2,1)S(1)}, bf16[288,896]{1,0:T(8,128)(2,1)S(1)}, u32[]{:S(2)}, u32[]{:S(2)}) collective-permute-start(bf16[288,896]{1,0:T(8,128)(2,1)S(1)} %get-tuple-element.57), channel_id=1, source_target_pairs={{0,6},{1,7},{2,0},{3,1},{4,2},{5,3},{6,4},{7,5},{8,10},{9,11},{10,... | collective-permute-start | bytes 1548296 | tf_op jit(solution)/shard_map/ppermute | solution.py:458
  138.8 13.6 %collective-permute-start.13 = (bf16[288,896]{1,0:T(8,128)(2,1)S(1)}, bf16[288,896]{1,0:T(8,128)(2,1)S(1)}, u32[]{:S(2)}, u32[]{:S(2)}) collective-permute-start(bf16[288,896]{1,0:T(8,128)(2,1)S(1)} %get-tuple-element.59), channel_id=1, source_target_pairs={{0,2},{1,3},{2,4},{3,5},{4,6},{5,7},{6,0},{7,1},{8,14},{9,15},{10,... | collective-permute-start | bytes 1548296 | tf_op jit(solution)/shard_map/ppermute | solution.py:458
  138.8 13.6 %copy-start.9 = (bf16[1024,1024]{1,0:T(8,128)(2,1)S(1)}, bf16[1024,1024]{1,0:T(8,128)(2,1)}, u32[]{:S(2)}) copy-start(bf16[1024,1024]{1,0:T(8,128)(2,1)} %copy-done.8) | copy-start | bytes 6291460
  156.0 33.8 %all-to-all-start.2 = ((bf16[64,112,128]{2,1,0:T(8,128)(2,1)}), bf16[64,112,128]{2,1,0:T(8,128)(2,1)S(1)}, u32[]{:S(2)}, u32[]{:S(2)}) async-start(bf16[64,112,128]{2,1,0:T(8,128)(2,1)} %bitcast.6), calls=%async_computation.2 | async-start | bytes 3670016 | tf_op jit(solution)/shard_map/all_to_all | solution.py:491
  172.3 3.4 %collective-permute-start.8 = (bf16[768,896]{1,0:T(8,128)(2,1)}, bf16[768,896]{1,0:T(8,128)(2,1)S(1)}, u32[]{:S(2)}, u32[]{:S(2)}) collective-permute-start(bf16[768,896]{1,0:T(8,128)(2,1)} %get-tuple-element.54), channel_id=1, source_target_pairs={{0,8},{8,0},{1,9},{9,1},{2,10},{10,2},{3,11},{11,3},{4,12},{12,4},... | collective-permute-start | bytes 4128776 | tf_op jit(solution)/shard_map/ppermute | solution.py:463
  175.8 14.0 %copy-start.16 = (f32[2,112,152]{1,2,0:T(8,128)S(1)}, f32[2,112,152]{1,2,0:T(8,128)}, u32[]{:S(2)}) copy-start(f32[2,112,152]{1,2,0:T(8,128)} %param.14) | copy-start | bytes 408580
  175.8 14.0 %copy-start.17 = (f32[152,112]{1,0:T(8,128)S(1)}, f32[152,112]{1,0:T(8,128)}, u32[]{:S(2)}) copy-start(f32[152,112]{1,0:T(8,128)} %refs_3_.1) | copy-start | bytes 204292
  175.8 14.0 %copy-start.18 = (f32[2,112,152]{1,2,0:T(8,128)S(1)}, f32[2,112,152]{1,2,0:T(8,128)}, u32[]{:S(2)}) copy-start(f32[2,112,152]{1,2,0:T(8,128)} %param.16) | copy-start | bytes 408580
  175.8 14.0 %copy-start.19 = (f32[2,112,152]{1,2,0:T(8,128)S(1)}, f32[2,112,152]{1,2,0:T(8,128)}, u32[]{:S(2)}) copy-start(f32[2,112,152]{1,2,0:T(8,128)} %param.17) | copy-start | bytes 408580
  175.8 14.0 %copy-start.20 = (f32[152,112]{1,0:T(8,128)S(1)}, f32[152,112]{1,0:T(8,128)}, u32[]{:S(2)}) copy-start(f32[152,112]{1,0:T(8,128)} %refs_4_.1) | copy-start | bytes 204292
  175.8 14.0 %copy-start.21 = (f32[152,112]{1,0:T(8,128)S(1)}, f32[152,112]{1,0:T(8,128)}, u32[]{:S(2)}) copy-start(f32[152,112]{1,0:T(8,128)} %refs_5_.1) | copy-start | bytes 204292
  (8 other events, 35.1 us)
where the time goes:
time: 192 us
  blocking collectives  78.5 us (41%)
  Pallas kernels  53.7 us (28%)
  waiting for transfers between devices  29.5 us (15%)
  starting transfers between devices  24.9 us (13%)
  other arithmetic  3.23 us (2%)
    all_to_all x1, blocking collectives, per_device(): slots = lax.all_to_all(slots, ('y', 'zh'), 0, 0, tiled=True)  46.2 us
    all_to_all x1, blocking collectives, per_device(): arrived = lax.all_to_all(packed, GROUP, 0, 0, tiled=True)  32.2 us
    pallas_call x4, Pallas kernels, one_part(): pl.pallas_call(part_kernel, out_shape=tuple((jax.ShapeDtypeStruct((3 * n,...  26.7 us
    ppermute x12, starting transfers between devices, shifted(): lax.ppermute(v, AXES, shift_pairs(sizes, stream, hops))  17.6 us
    ppermute x12, waiting for transfers between devices, shifted(): lax.ppermute(v, AXES, shift_pairs(sizes, stream, hops))  15.5 us
    all_to_all x1, waiting for transfers between devices, per_device(): pieces = lax.all_to_all(messages, GROUP, 0, 0, tiled=True)  10.7 us
    pallas_call x1, Pallas kernels, mix(): pl.pallas_call(mix_kernel, out_shape=(jax.ShapeDtypeStruct((rows, d), F32...  9.2 us
    all_to_all x1, starting transfers between devices, per_device(): pieces = lax.all_to_all(messages, GROUP, 0, 0, tiled=True)  7.18 us
  transfers between devices with their start and end apart: 15, of which 7 were waited for; matrix products, arithmetic and copies ran while one was open for 2% of the time, Pallas kernels for 20%

commit v1 on v0

--- a/solution.py
+++ b/solution.py
@@ -476,7 +476,7 @@
     packed, slots = lax.optimization_barrier((packed, slots))
     arrived = lax.all_to_all(packed, GROUP, 0, 0, tiled=True)
     own = assemble_weights(arrived.reshape(8, d, 128))
-    near_in = unpack(me, counts, owners, slots, cotangent, own[0])
+    near_in = unpack(me, counts, owners, slots, cotangent, me)
     *acts, rows_of = turn(near_in, swap_cores(near_in))
     weights = [shifted(own, -k) for k in HOPS] + [own]
     sums, hids, after = [], [], [near_in]

time: 192 us -> 187 us (0.974)
  blocking collectives: 78.5 us -> 46.2 us
  waiting for transfers between devices: 29.5 us -> 41.5 us
  starting transfers between devices: 24.9 us -> 34.5 us
  Pallas kernels: 53.7 us -> 57 us
  local copies, waits for them, and re-layouts: 1.04 us -> 3.26 us
    all_to_all x1 -> x0, blocking collectives: 32.2 us -> none  [per_device(): arrived = lax.all_to_all(packed, GROUP, 0, 0, tiled=True)]
    all_to_all x0 -> x1, waiting for transfers between devices: none -> 20.1 us  [per_device(): arrived = lax.all_to_all(packed, GROUP, 0, 0, tiled=True)]
    all_to_all x0 -> x1, starting transfers between devices: none -> 7.04 us  [per_device(): arrived = lax.all_to_all(packed, GROUP, 0, 0, tiled=True)]
    ppermute x12, waiting for transfers between devices: 15.5 us -> 11.3 us  [shifted(): lax.ppermute(v, AXES, shift_pairs(sizes, stream, hops))]
    all_to_all x1, waiting for transfers between devices: 10.7 us -> 6.77 us  [per_device(): pieces = lax.all_to_all(messages, GROUP, 0, 0, tiled=True)]
    ppermute x12, starting transfers between devices: 17.6 us -> 20.1 us  [shifted(): lax.ppermute(v, AXES, shift_pairs(sizes, stream, hops))]
    unnamed x50 -> x46, local copies, waits for them, and re-layouts: 1.04 us -> 3.26 us
  transfers between devices with their start and end apart: 15 -> 16, of which waited for: 7 -> 7; matrix products, arithmetic and copies ran while one was open for 2% -> 2% of each run, Pallas kernels for 20% -> 25%
where the time goes in v1:
time: 187 us
  Pallas kernels  57 us (30%)
  blocking collectives  46.2 us (25%)
  waiting for transfers between devices  41.5 us (22%)
  starting transfers between devices  34.5 us (18%)
  local copies, waits for them, and re-layouts  3.26 us (2%)
  other arithmetic  3.23 us (2%)
    all_to_all x1, blocking collectives, per_device(): slots = lax.all_to_all(slots, ('y', 'zh'), 0, 0, tiled=True)  46.2 us
    pallas_call x4, Pallas kernels, one_part(): pl.pallas_call(part_kernel, out_shape=tuple((jax.ShapeDtypeStruct((3 * n,...  26.7 us
    all_to_all x1, waiting for transfers between devices, per_device(): arrived = lax.all_to_all(packed, GROUP, 0, 0, tiled=True)  20.1 us
    ppermute x12, starting transfers between devices, shifted(): lax.ppermute(v, AXES, shift_pairs(sizes, stream, hops))  20.1 us
    ppermute x12, waiting for transfers between devices, shifted(): lax.ppermute(v, AXES, shift_pairs(sizes, stream, hops))  11.3 us
    pallas_call x1, Pallas kernels, mix(): pl.pallas_call(mix_kernel, out_shape=(jax.ShapeDtypeStruct((rows, d), F32...  9.21 us
    all_to_all x1, starting transfers between devices, per_device(): pieces = lax.all_to_all(messages, GROUP, 0, 0, tiled=True)  7.16 us
    all_to_all x1, starting transfers between devices, per_device(): arrived = lax.all_to_all(packed, GROUP, 0, 0, tiled=True)  7.04 us
  transfers between devices with their start and end apart: 16, of which 7 were waited for; matrix products, arithmetic and copies ran while one was open for 2% of the time, Pallas kernels for 25%

profile of v1, /device:TPU:0, one launch (start us, length us, event | category | flops | bytes accessed | tf_op | source)
XLA Modules:
  0.0 186.6 jit_solution(15561027445651377964)
XLA Ops:
  0.6 5.2 %shard_map.153 = (bf16[8,208,896]{2,1,0:T(8,128)(2,1)}, bf16[64,112,128]{2,1,0:T(8,128)(2,1)}) custom-call(s32[1]{0:T(128)} %bitcast.me_ref.after_ref, s32[1]{0:T(128)} %bitcast.3.core_ref, s32[8,8]{1,0:T(8,128)} %bitcast.16, s32[8,8]{1,0:T(8,128)} %bitcast.18, bf16[1536,896]{1,0:T(8,128)(2,1)} %x_ref.1, f32[2,152,112]{2,1,0:T(8,128)} %bitcast.12, ...), custom_call_target="tpu_custom_call" | custom-call | tf_op jit(solution)/shard_map/pallas_call | solution.py:157
  5.8 46.2 %all_to_all.15.slots_ref = bf16[8,208,896]{2,1,0:T(8,128)(2,1)} all-to-all(bf16[8,208,896]{2,1,0:T(8,128)(2,1)} %get-tuple-element.39), channel_id=1, replica_groups=mesh['x'=4,'zl'=2,'c'=2,'y'=4,'zh'=2] {'y','zh'}, dimensions={0} | all-to-all | bytes 5963776 | tf_op jit(solution)/shard_map/all_to_all | solution.py:475
  52.0 7.0 %all-to-all-start.1 = ((bf16[64,112,128]{2,1,0:T(8,128)(2,1)}), bf16[64,112,128]{2,1,0:T(8,128)(2,1)}, u32[]{:S(2)}, u32[]{:S(2)}) async-start(bf16[64,112,128]{2,1,0:T(8,128)(2,1)} %get-tuple-element.45), calls=%async_computation.1 | async-start | bytes 3670016 | tf_op jit(solution)/shard_map/all_to_all | solution.py:477
  59.1 1.8 copy-done.1
  60.9 1.3 copy-done.13
  62.2 2.2 %shard_map.154.a_ref.refs_0_.tok_ref = bf16[2,768,896]{2,1,0:T(8,128)(2,1)S(1)} custom-call(s32[1]{0:T(128)} %bitcast.me_ref.after_ref, s32[8,8]{1,0:T(8,128)S(1)} %bitcast.17, s32[8,8]{1,0:T(8,128)S(1)} %bitcast.19, bf16[8,208,896]{2,1,0:T(8,128)(2,1)S(1)} %copy-done.1, bf16[768,896]{1,0:T(8,128)(2,1)S(1)} %copy-done.13, s32[1]{0:T(128)} %bitcast.me_ref.after_ref), custom_call_target="tpu_custom_call" | custom-call | tf_op jit(solution)/shard_map/pallas_call | solution.py:206
  64.6 20.1 %all-to-all-done.1 = bf16[64,112,128]{2,1,0:T(8,128)(2,1)} async-done(((bf16[64,112,128]{2,1,0:T(8,128)(2,1)}), bf16[64,112,128]{2,1,0:T(8,128)(2,1)}, u32[]{:S(2)}, u32[]{:S(2)}) %all-to-all-start.1) | async-done | bytes 1835040 | tf_op jit(solution)/shard_map/all_to_all | solution.py:477
  84.7 3.6 %shard_map.156 = (bf16[624,896]{1,0:T(8,128)(2,1)S(1)}, bf16[288,896]{1,0:T(8,128)(2,1)S(1)}) custom-call(bf16[8,896,128]{2,1,0:T(8,128)(2,1)} %bitcast.5.a_ref), custom_call_target="tpu_custom_call" | custom-call | tf_op jit(solution)/shard_map/pallas_call | solution.py:259
  89.1 1.2 collective-permute-start.3
  90.3 2.0 %collective-permute-start.5 = (bf16[624,896]{1,0:T(8,128)(2,1)S(1)}, bf16[624,896]{1,0:T(8,128)(2,1)S(1)}, u32[]{:S(2)}, u32[]{:S(2)}) collective-permute-start(bf16[624,896]{1,0:T(8,128)(2,1)S(1)} %get-tuple-element.46.wx.refs_10_), channel_id=1, source_target_pairs={{0,96},{1,97},{2,98},{3,99},{4,100},{5,101},{6,102},{7,103},{8,24}... | collective-permute-start | bytes 3354632 | tf_op jit(solution)/shard_map/ppermute | solution.py:458
  92.3 1.6 collective-permute-start.2
  94.7 4.4 %shard_map.155 = (bf16[1536,896]{1,0:T(8,128)(2,1)S(1)}, bf16[896,1536]{1,0:T(8,128)(2,1)S(1)}, bf16[1536,896]{1,0:T(8,128)(2,1)S(1)}, bf16[896,1536]{1,0:T(8,128)(2,1)S(1)}, bf16[1024,1024]{1,0:T(8,128)(2,1)S(1)}) custom-call(bf16[2,768,896]{2,1,0:T(8,128)(2,1)S(1)} %shard_map.154.a_ref.refs_0_.tok_ref, bf16[2,768,896]{2,1,0:T(8,128)(2,1)} %collective-permute-done.b_ref), custom_call_target="tpu_custom_call" | custom-call | tf_op jit(solution)/shard_map/pallas_call | solution.py:242
  99.2 4.5 %collective-permute-done.2.wy.refs_5_ = bf16[288,896]{1,0:T(8,128)(2,1)S(1)} collective-permute-done((bf16[288,896]{1,0:T(8,128)(2,1)S(1)}, bf16[288,896]{1,0:T(8,128)(2,1)S(1)}, u32[]{:S(2)}, u32[]{:S(2)}) %collective-permute-start.2) | collective-permute-done | bytes 516128 | tf_op jit(solution)/shard_map/ppermute | solution.py:458
  103.6 6.4 %collective-permute-start.6 = (bf16[288,896]{1,0:T(8,128)(2,1)S(1)}, bf16[288,896]{1,0:T(8,128)(2,1)S(1)}, u32[]{:S(2)}, u32[]{:S(2)}) collective-permute-start(bf16[288,896]{1,0:T(8,128)(2,1)S(1)} %get-tuple-element.47.wy.refs_11_), channel_id=1, source_target_pairs={{0,6},{1,7},{2,0},{3,1},{4,2},{5,3},{6,4},{7,5},{8,10},{9,11},{10,... | collective-permute-start | bytes 1548296 | tf_op jit(solution)/shard_map/ppermute | solution.py:458
  110.1 6.7 %shard_map.157 = (bf16[624,896]{1,0:T(8,128)(2,1)S(1)}, bf16[288,896]{1,0:T(8,128)(2,1)S(1)}, bf16[304,1536]{1,0:T(8,128)(2,1)S(1)}) custom-call(bf16[1536,896]{1,0:T(8,128)(2,1)S(1)} %get-tuple-element.41.nrm, bf16[896,1536]{1,0:T(8,128)(2,1)S(1)} %get-tuple-element.42.nrm_t, bf16[1536,896]{1,0:T(8,128)(2,1)S(1)} %get-tuple-element.43.cot, ...), custom_call_target="tpu_custom_call" | custom-call | flops 200000000 | bytes 400000 | tf_op jit(solution)/shard_map/pallas_call | solution.py:303
  116.8 1.4 collective-permute-start.7
  118.2 1.2 collective-permute-start.9
  119.4 6.7 %shard_map.158 = (bf16[624,896]{1,0:T(8,128)(2,1)S(1)}, bf16[288,896]{1,0:T(8,128)(2,1)S(1)}, bf16[304,1536]{1,0:T(8,128)(2,1)S(1)}) custom-call(bf16[1536,896]{1,0:T(8,128)(2,1)S(1)} %get-tuple-element.41.nrm, bf16[896,1536]{1,0:T(8,128)(2,1)S(1)} %get-tuple-element.42.nrm_t, bf16[1536,896]{1,0:T(8,128)(2,1)S(1)} %get-tuple-element.43.cot, ...), custom_call_target="tpu_custom_call" | custom-call | flops 200000000 | bytes 400000 | tf_op jit(solution)/shard_map/pallas_call | solution.py:303
  126.1 1.4 collective-permute-start.10
  127.5 6.7 %shard_map.159 = (bf16[624,896]{1,0:T(8,128)(2,1)S(1)}, bf16[288,896]{1,0:T(8,128)(2,1)S(1)}, bf16[304,1536]{1,0:T(8,128)(2,1)S(1)}) custom-call(bf16[1536,896]{1,0:T(8,128)(2,1)S(1)} %get-tuple-element.41.nrm, bf16[896,1536]{1,0:T(8,128)(2,1)S(1)} %get-tuple-element.42.nrm_t, bf16[1536,896]{1,0:T(8,128)(2,1)S(1)} %get-tuple-element.43.cot, ...), custom_call_target="tpu_custom_call" | custom-call | flops 200000000 | bytes 400000 | tf_op jit(solution)/shard_map/pallas_call | solution.py:303
  135.0 2.5 %collective-permute-start.11 = (bf16[288,896]{1,0:T(8,128)(2,1)S(1)}, bf16[288,896]{1,0:T(8,128)(2,1)S(1)}, u32[]{:S(2)}, u32[]{:S(2)}) collective-permute-start(bf16[288,896]{1,0:T(8,128)(2,1)S(1)} %get-tuple-element.57), channel_id=1, source_target_pairs={{0,6},{1,7},{2,0},{3,1},{4,2},{5,3},{6,4},{7,5},{8,10},{9,11},{10,... | collective-permute-start | bytes 1548296 | tf_op jit(solution)/shard_map/ppermute | solution.py:458
  137.5 6.7 %shard_map.160 = (bf16[624,896]{1,0:T(8,128)(2,1)S(1)}, bf16[288,896]{1,0:T(8,128)(2,1)S(1)}, bf16[304,1536]{1,0:T(8,128)(2,1)S(1)}) custom-call(bf16[1536,896]{1,0:T(8,128)(2,1)S(1)} %get-tuple-element.41.nrm, bf16[896,1536]{1,0:T(8,128)(2,1)S(1)} %get-tuple-element.42.nrm_t, bf16[1536,896]{1,0:T(8,128)(2,1)S(1)} %get-tuple-element.43.cot, ...), custom_call_target="tpu_custom_call" | custom-call | flops 200000000 | bytes 400000 | tf_op jit(solution)/shard_map/pallas_call | solution.py:303
  144.2 0.9 collective-permute-done.11.refs_3_
  145.2 2.7 %collective-permute-done.13.refs_5_ = bf16[288,896]{1,0:T(8,128)(2,1)S(1)} collective-permute-done((bf16[288,896]{1,0:T(8,128)(2,1)S(1)}, bf16[288,896]{1,0:T(8,128)(2,1)S(1)}, u32[]{:S(2)}, u32[]{:S(2)}) %collective-permute-start.13) | collective-permute-done | bytes 516128 | tf_op jit(solution)/shard_map/ppermute | solution.py:458
  147.8 3.2 %collective-permute-done.12.refs_4_ = bf16[624,896]{1,0:T(8,128)(2,1)S(1)} collective-permute-done((bf16[624,896]{1,0:T(8,128)(2,1)S(1)}, bf16[624,896]{1,0:T(8,128)(2,1)S(1)}, u32[]{:S(2)}, u32[]{:S(2)}) %collective-permute-start.12) | collective-permute-done | bytes 1118240 | tf_op jit(solution)/shard_map/ppermute | solution.py:458
  151.0 3.5 %shard_map.162 = bf16[8,896,128]{2,1,0:T(8,128)(2,1)} custom-call(bf16[624,896]{1,0:T(8,128)(2,1)S(1)} %collective-permute-done.9.refs_0_, bf16[288,896]{1,0:T(8,128)(2,1)S(1)} %collective-permute-done.7.refs_1_, bf16[624,896]{1,0:T(8,128)(2,1)S(1)} %collective-permute-done.10.refs_2_, bf16[288,896]{1,0:T(8,128)(2,1)S(1)} %collective-permute-done.11.refs_3_, ...), custom_call_target="tpu_custom_call" | custom-call | tf_op jit(solution)/shard_map/pallas_call | solution.py:383
  154.6 7.2 %all-to-all-start.2 = ((bf16[64,112,128]{2,1,0:T(8,128)(2,1)}), bf16[64,112,128]{2,1,0:T(8,128)(2,1)S(1)}, u32[]{:S(2)}, u32[]{:S(2)}) async-start(bf16[64,112,128]{2,1,0:T(8,128)(2,1)} %bitcast.6), calls=%async_computation.2 | async-start | bytes 3670016 | tf_op jit(solution)/shard_map/all_to_all | solution.py:491
  161.7 9.2 %shard_map.161 = (f32[768,896]{1,0:T(8,128)}, bf16[768,896]{1,0:T(8,128)(2,1)}) custom-call(bf16[2,768,896]{2,1,0:T(8,128)(2,1)} %copy-done, bf16[304,1536]{1,0:T(8,128)(2,1)} %copy-done.6, bf16[304,1536]{1,0:T(8,128)(2,1)} %copy-done.7, bf16[304,1536]{1,0:T(8,128)(2,1)} %copy-done.8, bf16[304,1536]{1,0:T(8,128)(2,1)} %copy-done.14, ...), custom_call_target="tpu_custom_call" | custom-call | flops 3500000000 | bytes 16000000 | tf_op jit(solution)/shard_map/pallas_call | solution.py:347
  171.0 3.3 %collective-permute-done.8 = bf16[768,896]{1,0:T(8,128)(2,1)S(1)} collective-permute-done((bf16[768,896]{1,0:T(8,128)(2,1)}, bf16[768,896]{1,0:T(8,128)(2,1)S(1)}, u32[]{:S(2)}, u32[]{:S(2)}) %collective-permute-start.8) | collective-permute-done | bytes 1376288 | tf_op jit(solution)/shard_map/ppermute | solution.py:463
  174.4 3.2 %add_convert_fusion = bf16[768,896]{1,0:T(8,128)(2,1)} fusion(f32[768,896]{1,0:T(8,128)} %get-tuple-element.53, bf16[768,896]{1,0:T(8,128)(2,1)S(1)} %collective-permute-done.8), kind=kLoop, calls=%fused_computation | loop fusion | flops 2064384 | bytes 5505024 | tf_op jit(solution)/shard_map/convert_element_type | solution.py:493
  177.6 6.8 %all-to-all-done.2.a_ref = bf16[64,112,128]{2,1,0:T(8,128)(2,1)S(1)} async-done(((bf16[64,112,128]{2,1,0:T(8,128)(2,1)}), bf16[64,112,128]{2,1,0:T(8,128)(2,1)S(1)}, u32[]{:S(2)}, u32[]{:S(2)}) %all-to-all-start.2) | async-done | bytes 1835040 | tf_op jit(solution)/shard_map/all_to_all | solution.py:491
  184.5 2.1 %shard_map.163 = (f32[2,152,112]{2,1,0:T(8,128)}, f32[2,152,112]{2,1,0:T(8,128)}, f32[2,152,112]{2,1,0:T(8,128)}, f32[152,112]{1,0:T(8,128)}, f32[152,112]{1,0:T(8,128)}, /*index=5*/f32[152,112]{1,0:T(8,128)}) custom-call(s32[1]{0:T(128)} %bitcast.3.core_ref, bf16[64,112,128]{2,1,0:T(8,128)(2,1)S(1)} %all-to-all-done.2.a_ref, f32[2,152,112]{2,1,0:T(8,128)S(1)} %bitcast.13, ...), custom_call_target="tpu_custom_call" | custom-call | tf_op jit(solution)/shard_map/pallas_call | solution.py:423
  (59 shorter events, 2.6 us)
Async XLA Ops:
  52.0 7.1 %copy-start.22 = (s32[1,8,8]{2,1,0:T(8,128)S(1)}, s32[1,8,8]{2,1,0:T(8,128)}, u32[]{:S(2)}) copy-start(s32[1,8,8]{2,1,0:T(8,128)} %param.13) | copy-start | bytes 772
  52.0 32.7 %all-to-all-start.1 = ((bf16[64,112,128]{2,1,0:T(8,128)(2,1)}), bf16[64,112,128]{2,1,0:T(8,128)(2,1)}, u32[]{:S(2)}, u32[]{:S(2)}) async-start(bf16[64,112,128]{2,1,0:T(8,128)(2,1)} %get-tuple-element.45), calls=%async_computation.1 | async-start | bytes 3670016 | tf_op jit(solution)/shard_map/all_to_all | solution.py:477
  64.5 45.6 %copy-start = (bf16[2,768,896]{2,1,0:T(8,128)(2,1)}, bf16[2,768,896]{2,1,0:T(8,128)(2,1)S(1)}, u32[]{:S(2)}) copy-start(bf16[2,768,896]{2,1,0:T(8,128)(2,1)S(1)} %shard_map.154.a_ref.refs_0_.tok_ref) | copy-start | bytes 8257540
  64.5 29.5 %collective-permute-start = (bf16[2,768,896]{2,1,0:T(8,128)(2,1)S(1)}, bf16[2,768,896]{2,1,0:T(8,128)(2,1)}, u32[]{:S(2)}, u32[]{:S(2)}) collective-permute-start(bf16[2,768,896]{2,1,0:T(8,128)(2,1)S(1)} %shard_map.154.a_ref.refs_0_.tok_ref), channel_id=1, source_target_pairs={{0,8},{8,0},{1,9},{9,1},{2,10},{10,2},{3,11},{11,3},{4,12},{12,4},... | collective-permute-start | bytes 8257544 | tf_op jit(solution)/shard_map/ppermute | solution.py:463
  88.3 49.2 %copy-start.2 = (bf16[624,896]{1,0:T(8,128)(2,1)}, bf16[624,896]{1,0:T(8,128)(2,1)S(1)}, u32[]{:S(2)}) copy-start(bf16[624,896]{1,0:T(8,128)(2,1)S(1)} %get-tuple-element.46.wx.refs_10_) | copy-start | bytes 3354628
  88.3 49.2 %copy-start.9 = (bf16[288,896]{1,0:T(8,128)(2,1)}, bf16[288,896]{1,0:T(8,128)(2,1)S(1)}, u32[]{:S(2)}) copy-start(bf16[288,896]{1,0:T(8,128)(2,1)S(1)} %get-tuple-element.47.wy.refs_11_) | copy-start | bytes 1548292
  88.3 21.7 %collective-permute-start.1 = (bf16[624,896]{1,0:T(8,128)(2,1)S(1)}, bf16[624,896]{1,0:T(8,128)(2,1)S(1)}, u32[]{:S(2)}, u32[]{:S(2)}) collective-permute-start(bf16[624,896]{1,0:T(8,128)(2,1)S(1)} %get-tuple-element.46.wx.refs_10_), channel_id=1, source_target_pairs={{0,64},{1,65},{2,66},{3,67},{4,68},{5,69},{6,70},{7,71},{8,9},{9,8... | collective-permute-start | bytes 3354632 | tf_op jit(solution)/shard_map/ppermute | solution.py:458
  89.1 30.3 %collective-permute-start.3 = (bf16[624,896]{1,0:T(8,128)(2,1)S(1)}, bf16[624,896]{1,0:T(8,128)(2,1)S(1)}, u32[]{:S(2)}, u32[]{:S(2)}) collective-permute-start(bf16[624,896]{1,0:T(8,128)(2,1)S(1)} %get-tuple-element.46.wx.refs_10_), channel_id=1, source_target_pairs={{0,32},{1,33},{2,34},{3,35},{4,36},{5,37},{6,38},{7,39},{8,25},{9,... | collective-permute-start | bytes 3354632 | tf_op jit(solution)/shard_map/ppermute | solution.py:458
  90.3 37.1 %collective-permute-start.5 = (bf16[624,896]{1,0:T(8,128)(2,1)S(1)}, bf16[624,896]{1,0:T(8,128)(2,1)S(1)}, u32[]{:S(2)}, u32[]{:S(2)}) collective-permute-start(bf16[624,896]{1,0:T(8,128)(2,1)S(1)} %get-tuple-element.46.wx.refs_10_), channel_id=1, source_target_pairs={{0,96},{1,97},{2,98},{3,99},{4,100},{5,101},{6,102},{7,103},{8,24}... | collective-permute-start | bytes 3354632 | tf_op jit(solution)/shard_map/ppermute | solution.py:458
  92.3 11.3 %collective-permute-start.2 = (bf16[288,896]{1,0:T(8,128)(2,1)S(1)}, bf16[288,896]{1,0:T(8,128)(2,1)S(1)}, u32[]{:S(2)}, u32[]{:S(2)}) collective-permute-start(bf16[288,896]{1,0:T(8,128)(2,1)S(1)} %get-tuple-element.47.wy.refs_11_), channel_id=1, source_target_pairs={{0,4},{1,5},{2,6},{3,7},{4,0},{5,1},{6,2},{7,3},{8,12},{9,13},{10,... | collective-permute-start | bytes 1548296 | tf_op jit(solution)/shard_map/ppermute | solution.py:458
  94.0 24.2 %collective-permute-start.4 = (bf16[288,896]{1,0:T(8,128)(2,1)S(1)}, bf16[288,896]{1,0:T(8,128)(2,1)S(1)}, u32[]{:S(2)}, u32[]{:S(2)}) collective-permute-start(bf16[288,896]{1,0:T(8,128)(2,1)S(1)} %get-tuple-element.47.wy.refs_11_), channel_id=1, source_target_pairs={{0,2},{1,3},{2,4},{3,5},{4,6},{5,7},{6,0},{7,1},{8,14},{9,15},{10,... | collective-permute-start | bytes 1548296 | tf_op jit(solution)/shard_map/ppermute | solution.py:458
  103.6 13.1 %copy-start.10 = (bf16[288,896]{1,0:T(8,128)(2,1)}, bf16[288,896]{1,0:T(8,128)(2,1)S(1)}, u32[]{:S(2)}) copy-start(bf16[288,896]{1,0:T(8,128)(2,1)S(1)} %collective-permute-done.2.wy.refs_5_) | copy-start | bytes 1548292
  103.6 23.8 %collective-permute-start.6 = (bf16[288,896]{1,0:T(8,128)(2,1)S(1)}, bf16[288,896]{1,0:T(8,128)(2,1)S(1)}, u32[]{:S(2)}, u32[]{:S(2)}) collective-permute-start(bf16[288,896]{1,0:T(8,128)(2,1)S(1)} %get-tuple-element.47.wy.refs_11_), channel_id=1, source_target_pairs={{0,6},{1,7},{2,0},{3,1},{4,2},{5,3},{6,4},{7,5},{8,10},{9,11},{10,... | collective-permute-start | bytes 1548296 | tf_op jit(solution)/shard_map/ppermute | solution.py:458
  116.8 9.3 %copy-start.6 = (bf16[304,1536]{1,0:T(8,128)(2,1)}, bf16[304,1536]{1,0:T(8,128)(2,1)S(1)}, u32[]{:S(2)}) copy-start(bf16[304,1536]{1,0:T(8,128)(2,1)S(1)} %get-tuple-element.48.refs_0_) | copy-start | bytes 2801668
  116.8 10.7 %collective-permute-start.7 = (bf16[288,896]{1,0:T(8,128)(2,1)S(1)}, bf16[288,896]{1,0:T(8,128)(2,1)S(1)}, u32[]{:S(2)}, u32[]{:S(2)}) collective-permute-start(bf16[288,896]{1,0:T(8,128)(2,1)S(1)} %get-tuple-element.50), channel_id=1, source_target_pairs={{0,4},{1,5},{2,6},{3,7},{4,0},{5,1},{6,2},{7,3},{8,12},{9,13},{10,... | collective-permute-start | bytes 1548296 | tf_op jit(solution)/shard_map/ppermute | solution.py:458
  118.2 7.9 %copy-start.11 = (bf16[288,896]{1,0:T(8,128)(2,1)}, bf16[288,896]{1,0:T(8,128)(2,1)S(1)}, u32[]{:S(2)}) copy-start(bf16[288,896]{1,0:T(8,128)(2,1)S(1)} %collective-permute-done.4.wy.refs_7_) | copy-start | bytes 1548292
  118.2 29.6 %collective-permute-start.9 = (bf16[624,896]{1,0:T(8,128)(2,1)S(1)}, bf16[624,896]{1,0:T(8,128)(2,1)S(1)}, u32[]{:S(2)}, u32[]{:S(2)}) collective-permute-start(bf16[624,896]{1,0:T(8,128)(2,1)S(1)} %get-tuple-element.55), channel_id=1, source_target_pairs={{0,64},{1,65},{2,66},{3,67},{4,68},{5,69},{6,70},{7,71},{8,9},{9,8... | collective-permute-start | bytes 3354632 | tf_op jit(solution)/shard_map/ppermute | solution.py:458
  126.1 8.1 %copy-start.7 = (bf16[304,1536]{1,0:T(8,128)(2,1)}, bf16[304,1536]{1,0:T(8,128)(2,1)S(1)}, u32[]{:S(2)}) copy-start(bf16[304,1536]{1,0:T(8,128)(2,1)S(1)} %get-tuple-element.49.refs_0_.refs_1_) | copy-start | bytes 2801668
  126.1 21.7 %collective-permute-start.10 = (bf16[624,896]{1,0:T(8,128)(2,1)S(1)}, bf16[624,896]{1,0:T(8,128)(2,1)S(1)}, u32[]{:S(2)}, u32[]{:S(2)}) collective-permute-start(bf16[624,896]{1,0:T(8,128)(2,1)S(1)} %get-tuple-element.56), channel_id=1, source_target_pairs={{0,96},{1,97},{2,98},{3,99},{4,100},{5,101},{6,102},{7,103},{8,24}... | collective-permute-start | bytes 3354632 | tf_op jit(solution)/shard_map/ppermute | solution.py:458
  134.2 10.0 %copy-start.8 = (bf16[304,1536]{1,0:T(8,128)(2,1)}, bf16[304,1536]{1,0:T(8,128)(2,1)S(1)}, u32[]{:S(2)}) copy-start(bf16[304,1536]{1,0:T(8,128)(2,1)S(1)} %get-tuple-element.51.refs_0_.refs_2_) | copy-start | bytes 2801668
  134.2 16.8 %collective-permute-start.12 = (bf16[624,896]{1,0:T(8,128)(2,1)S(1)}, bf16[624,896]{1,0:T(8,128)(2,1)S(1)}, u32[]{:S(2)}, u32[]{:S(2)}) collective-permute-start(bf16[624,896]{1,0:T(8,128)(2,1)S(1)} %get-tuple-element.58), channel_id=1, source_target_pairs={{0,32},{1,33},{2,34},{3,35},{4,36},{5,37},{6,38},{7,39},{8,25},{9,... | collective-permute-start | bytes 3354632 | tf_op jit(solution)/shard_map/ppermute | solution.py:458
  135.0 10.2 %collective-permute-start.11 = (bf16[288,896]{1,0:T(8,128)(2,1)S(1)}, bf16[288,896]{1,0:T(8,128)(2,1)S(1)}, u32[]{:S(2)}, u32[]{:S(2)}) collective-permute-start(bf16[288,896]{1,0:T(8,128)(2,1)S(1)} %get-tuple-element.57), channel_id=1, source_target_pairs={{0,6},{1,7},{2,0},{3,1},{4,2},{5,3},{6,4},{7,5},{8,10},{9,11},{10,... | collective-permute-start | bytes 1548296 | tf_op jit(solution)/shard_map/ppermute | solution.py:458
  137.5 10.3 %collective-permute-start.13 = (bf16[288,896]{1,0:T(8,128)(2,1)S(1)}, bf16[288,896]{1,0:T(8,128)(2,1)S(1)}, u32[]{:S(2)}, u32[]{:S(2)}) collective-permute-start(bf16[288,896]{1,0:T(8,128)(2,1)S(1)} %get-tuple-element.59), channel_id=1, source_target_pairs={{0,2},{1,3},{2,4},{3,5},{4,6},{5,7},{6,0},{7,1},{8,14},{9,15},{10,... | collective-permute-start | bytes 1548296 | tf_op jit(solution)/shard_map/ppermute | solution.py:458
  144.2 10.4 %copy-start.14 = (bf16[304,1536]{1,0:T(8,128)(2,1)}, bf16[304,1536]{1,0:T(8,128)(2,1)S(1)}, u32[]{:S(2)}) copy-start(bf16[304,1536]{1,0:T(8,128)(2,1)S(1)} %get-tuple-element.52.refs_3_) | copy-start | bytes 2801668
  154.6 29.8 %all-to-all-start.2 = ((bf16[64,112,128]{2,1,0:T(8,128)(2,1)}), bf16[64,112,128]{2,1,0:T(8,128)(2,1)S(1)}, u32[]{:S(2)}, u32[]{:S(2)}) async-start(bf16[64,112,128]{2,1,0:T(8,128)(2,1)} %bitcast.6), calls=%async_computation.2 | async-start | bytes 3670016 | tf_op jit(solution)/shard_map/all_to_all | solution.py:491
  171.0 3.4 %collective-permute-start.8 = (bf16[768,896]{1,0:T(8,128)(2,1)}, bf16[768,896]{1,0:T(8,128)(2,1)S(1)}, u32[]{:S(2)}, u32[]{:S(2)}) collective-permute-start(bf16[768,896]{1,0:T(8,128)(2,1)} %get-tuple-element.54), channel_id=1, source_target_pairs={{0,8},{8,0},{1,9},{9,1},{2,10},{10,2},{3,11},{11,3},{4,12},{12,4},... | collective-permute-start | bytes 4128776 | tf_op jit(solution)/shard_map/ppermute | solution.py:463
  174.4 10.0 %copy-start.15 = (f32[2,112,152]{1,2,0:T(8,128)S(1)}, f32[2,112,152]{1,2,0:T(8,128)}, u32[]{:S(2)}) copy-start(f32[2,112,152]{1,2,0:T(8,128)} %param.14) | copy-start | bytes 408580
  174.4 10.0 %copy-start.16 = (f32[152,112]{1,0:T(8,128)S(1)}, f32[152,112]{1,0:T(8,128)}, u32[]{:S(2)}) copy-start(f32[152,112]{1,0:T(8,128)} %refs_3_.1) | copy-start | bytes 204292
  174.4 10.0 %copy-start.17 = (f32[2,112,152]{1,2,0:T(8,128)S(1)}, f32[2,112,152]{1,2,0:T(8,128)}, u32[]{:S(2)}) copy-start(f32[2,112,152]{1,2,0:T(8,128)} %param.16) | copy-start | bytes 408580
  174.4 10.0 %copy-start.18 = (f32[2,112,152]{1,2,0:T(8,128)S(1)}, f32[2,112,152]{1,2,0:T(8,128)}, u32[]{:S(2)}) copy-start(f32[2,112,152]{1,2,0:T(8,128)} %param.17) | copy-start | bytes 408580
  174.4 10.1 %copy-start.19 = (f32[152,112]{1,0:T(8,128)S(1)}, f32[152,112]{1,0:T(8,128)}, u32[]{:S(2)}) copy-start(f32[152,112]{1,0:T(8,128)} %refs_4_.1) | copy-start | bytes 204292
  174.4 10.1 %copy-start.20 = (f32[152,112]{1,0:T(8,128)S(1)}, f32[152,112]{1,0:T(8,128)}, u32[]{:S(2)}) copy-start(f32[152,112]{1,0:T(8,128)} %refs_5_.1) | copy-start | bytes 204292
  (7 other events, 37.1 us)
